TPU v7x, 512 devices: a whole 4x4x16 slice. The times are simulated.
512 devices in a mesh: band: 16 (over z_lo, x), head: 8 (over z_hi, core), member: 4 (over y).
Axes of the slice: x: 4, y: 4, z: 16 (z_hi: 4, z_lo: 4; z = z_hi * 4 + z_lo), core: 2. Of those that a mesh axis runs over, the one named last changes fastest.
Arguments:
- tokens: bfloat16 [229376, 1024], P(('member', 'band')), parts along dimension 0, may hold values from -48 to 48
- ln_gain: float32 [1024], replicated, may hold values from 0.1 to 1.9
- qkv_weight: bfloat16 [1024, 3, 1024], P(None, None, 'head'), may hold values from -0.1875 to 0.1875
- qk_gain: float32 [2, 16, 64], P(None, 'head'), may hold values from 0.1 to 1.9
- out_weight: bfloat16 [1024, 1024], replicated, may hold values from -0.1875 to 0.1875
- key_start: int32 [448], P('band'), may hold values from 0 to 446, as said below
- key_count: int32 [448], P('band'), may hold values from 2 to 15, as said below
Outputs:
- updated: bfloat16 [229376, 1024], P(('member', 'band', 'head')), parts along dimension 0
There are 4 independent parts, one for each index of `member`. A program takes and returns all parts, laid end to end along the dimension named above; an argument that names none is the same for every part. Nothing has to cross between parts.
Inputs may be any that keep to these rules, and one draw needn't show every extreme that they name: Query block b's window begins at key block key_start[b], where b - 7 <= key_start[b] <= b. The window of query block b ends at key block key_start[b] + key_count[b] - 1, which is at least b, at most b + 7, and at most the last block.
All inputs are finite; a program needn't handle non-finite values.
Results may differ from a plain program's by a relative error of at most 0.0034.
Values may be sent and summed in bfloat16 or wider, within the bound.
A program may use at most 128 MiB of HBM per device.

v0:
```python
import jax
import jax.numpy as jnp
from jax import lax
from jax.sharding import PartitionSpec as P

BLOCK = 128
REACH = 7


def extended(cells, sides, width):
    for axis, dim in sides:
        count = lax.axis_size(axis)
        ends = count - 1
        head = lax.slice_in_dim(cells, 0, width, axis=dim)
        tail = lax.slice_in_dim(cells, cells.shape[dim] - width, cells.shape[dim], axis=dim)
        cells = jnp.concatenate(
            [
                lax.ppermute(tail, axis, [(i, (i + 1) % count) for i in range(ends)]),
                cells,
                lax.ppermute(head, axis, [((i + 1) % count, i) for i in range(ends)]),
            ],
            axis=dim,
        )
    return cells


def layer_normed(tokens, ln_gain):
    values = tokens.astype(jnp.float32)
    center = jnp.mean(values, axis=-1, keepdims=True)
    spread = jnp.mean(jnp.square(values - center), axis=-1, keepdims=True)
    return ((values - center) * lax.rsqrt(spread + 1e-05) * ln_gain).astype(jnp.bfloat16)


def head_normed(values, gains):
    inverse = lax.rsqrt(jnp.mean(jnp.square(values), axis=-1, keepdims=True) + 1e-06)
    return (values * inverse * gains).astype(jnp.bfloat16)


def project_queries(feature_rows, weight_flat, qk_gain):
    head_count, head_size = (qk_gain.shape[1], qk_gain.shape[2])
    columns = head_count * head_size
    raw = jnp.dot(feature_rows, weight_flat[:, :columns], preferred_element_type=jnp.float32)
    raw = raw.reshape(feature_rows.shape[0], head_count, head_size)
    return head_normed(raw, qk_gain[0]).reshape(feature_rows.shape[0], columns)


def project_keys(feature_rows, weight_flat, qk_gain):
    head_count, head_size = (qk_gain.shape[1], qk_gain.shape[2])
    columns = head_count * head_size
    raw = jnp.dot(feature_rows, weight_flat[:, columns:], preferred_element_type=jnp.float32)
    key_part = raw[:, :columns].reshape(feature_rows.shape[0], head_count, head_size)
    key_part = head_normed(key_part, qk_gain[1]).reshape(feature_rows.shape[0], columns)
    value_part = raw[:, columns:].astype(jnp.bfloat16)
    return jnp.concatenate([key_part, value_part], axis=1)


def attend(query_rows, starts, counts, kv_ext, anchor, head_count, head_size):
    num_blocks = starts.shape[0]
    row_total = num_blocks * BLOCK
    span = (2 * REACH + 1) * BLOCK
    kv_padded = jnp.concatenate([kv_ext, jnp.zeros((span, kv_ext.shape[1]), kv_ext.dtype)], axis=0)
    query_heads = jnp.transpose(query_rows.reshape(row_total, head_count, head_size), (1, 0, 2))
    kv_heads = jnp.transpose(kv_padded.reshape(-1, 2, head_count, head_size), (1, 2, 0, 3))
    key_heads = kv_heads[0]
    value_heads = kv_heads[1]
    local_first = starts - anchor
    scale = head_size ** (-0.5)
    positions = jnp.arange(span, dtype=jnp.int32)

    def one_block(block_index):
        query_block = lax.dynamic_slice_in_dim(query_heads, block_index * BLOCK, BLOCK, 1)
        first_row = local_first[block_index] * BLOCK
        key_window = lax.dynamic_slice_in_dim(key_heads, first_row, span, 1)
        value_window = lax.dynamic_slice_in_dim(value_heads, first_row, span, 1)
        scores = (
            jnp.einsum("hid,hjd->hij", query_block, key_window, preferred_element_type=jnp.float32)
            * scale
        )
        live = positions < counts[block_index] * BLOCK
        weights = jnp.where(live[None, None, :], jnp.exp(scores), 0.0)
        totals = jnp.sum(weights, axis=-1)
        weighted = jnp.einsum(
            "hij,hjd->hid",
            weights.astype(jnp.bfloat16),
            value_window,
            preferred_element_type=jnp.float32,
        )
        finished = (weighted / totals[:, :, None]).astype(jnp.bfloat16)
        return jnp.transpose(finished, (1, 0, 2)).reshape(BLOCK, head_count * head_size)

    result = lax.map(one_block, jnp.arange(num_blocks, dtype=jnp.int32))
    return result.reshape(row_total, head_count * head_size)


def on_device(tokens, ln_gain, qkv_weight, qk_gain, out_weight, key_start, key_count):
    tok_rows, feature_count = tokens.shape
    head_count, head_size = (qk_gain.shape[1], qk_gain.shape[2])
    num_blocks = tok_rows // BLOCK
    band_pos = lax.axis_index("band")
    weight_flat = qkv_weight.reshape(feature_count, 3 * head_count * head_size)
    normed = layer_normed(tokens, ln_gain)
    queries = project_queries(normed, weight_flat, qk_gain)
    kv_local = project_keys(normed, weight_flat, qk_gain)
    kv_ext = extended(kv_local, (("band", 0),), REACH * BLOCK)
    anchor = band_pos * num_blocks - REACH
    attended = attend(queries, key_start, key_count, kv_ext, anchor, head_count, head_size)
    share = tok_rows // lax.axis_size("head")
    head_pos = lax.axis_index("head")
    residual_rows = lax.dynamic_slice_in_dim(tokens, head_pos * share, share, 0).astype(jnp.float32)
    all_heads = lax.all_to_all(attended, "head", split_axis=0, concat_axis=1, tiled=True)
    summed = jnp.dot(all_heads, out_weight, preferred_element_type=jnp.float32)
    return (residual_rows + summed).astype(jnp.bfloat16)


def solution(mesh):
    placed = (
        P(("member", "band"), None),
        P(),
        P(None, None, "head"),
        P(None, "head", None),
        P(),
        P("band"),
        P("band"),
    )
    return jax.shard_map(
        on_device,
        mesh=mesh,
        in_specs=placed,
        out_specs=P(("member", "band", "head"), None),
        check_vma=False,
    )
```

profile of v0, /device:TPU:10, one launch (start us, length us, event | category | flops | bytes accessed | tf_op | source)
XLA Modules:
  0.0 375.8 jit_solution(13899933798274751676)
XLA Ops:
  0.0 4.3 %convert_reduce_fusion = f32[3584]{0:T(1024)S(1)} fusion(bf16[3584,1024]{1,0:T(8,128)(2,1)} %param.9), kind=kLoop, calls=%fused_computation.16 | loop fusion | flops 7336448 | bytes 7354368 | tf_op jit(solution)/shard_map/reduce_sum | solution.py:29
  5.3 2.1 fusion.14
  8.9 5.4 %fusion.16 = bf16[3584,1024]{1,0:T(8,128)(2,1)S(1)} fusion(bf16[3584,1024]{1,0:T(8,128)(2,1)} %param.9, f32[1024]{0:T(1024)S(1)} %copy-done.6, f32[3584]{0:T(1024)S(1)} %add_rsqrt_fusion.2, f32[3584]{0:T(1024)S(1)} %broadcast_multiply_fusion), kind=kLoop, calls=%fused_computation.21 | loop fusion | flops 18350080 | bytes 14712832 | tf_op jit(solution)/shard_map/convert_element_type | solution.py:31
  14.3 2.1 fusion.22
  17.3 1.8 copy-done.4
  19.4 1.7 fusion.18
  22.3 2.4 collective-permute-start.1
  24.7 3.6 collective-permute-start
  28.3 5.6 %multiply_reduce_fusion = (f32[3584,2]{0,1:T(2,128)S(1)}, f32[3584,128]{0,1:T(8,128)S(1)}) fusion(bf16[3584,1024]{1,0:T(8,128)(2,1)} %copy-done.2, bf16[1024,384]{0,1:T(8,128)(2,1)} %bitcast.64), kind=kOutput, calls=%fused_computation.32 | convolution fusion | flops 940434432 | bytes 9465856 | tf_op jit(solution)/shard_map/dot_general | solution.py:42
  36.6 2.3 collective-permute-done
  38.9 6.0 %maximum_maximum_fusion = bf16[7296,256]{0,1:T(8,128)(2,1)S(1)} fusion(bf16[896,256]{0,1:T(8,128)(2,1)S(1)} %collective-permute-done.1, bf16[3584,128]{0,1:T(8,128)(2,1)S(1)} %slice.59, bf16[3584,128]{0,1:T(8,128)(2,1)} %copy-done.3, bf16[896,256]{0,1:T(8,128)(2,1)} %collective-permute-done, bf16[7296]{0:T(1024)(128)(2,1)S(1)} %pad.4.clone), kind=kLoop, calls=%fused_computation.22 | loop fusion | flops 18677760 | bytes 6502656 | tf_op jit(solution)/shard_map/concatenate | solution.py:61
  45.0 2.1 slice_bitcast_fusion
  47.0 259.1 %while.11 = (s32[]{:T(128)}, bf16[28,128,128]{2,1,0:T(8,128)(2,1)}, s32[28]{0:T(128)S(1)}, s32[28]{0:T(128)S(1)}, bf16[2,3584,64]{1,2,0:T(8,128)(2,1)}, /*index=...) while((s32[]{:T(128)}, bf16[28,128,128]{2,1,0:T(8,128)(2,1)}, ...), condition=%wide.region_6.7_spmd.clone, body=%wide.region_4.6_spmd.clone.sunk | while | flops 127829648 | bytes 3151959 | solution.py:91
  52.3 1.7 fusion.39
  61.6 1.7 fusion.39
  70.8 1.7 fusion.39
  80.1 1.7 fusion.39
  81.8 1.5 fusion.40
  89.3 1.7 fusion.39
  91.0 1.5 fusion.40
  98.6 1.7 fusion.39
  100.3 1.5 fusion.40
  107.8 1.7 fusion.39
  109.6 1.5 fusion.40
  117.1 1.7 fusion.39
  126.4 1.7 fusion.39
  135.6 1.7 fusion.39
  144.9 1.7 fusion.39
  154.1 1.7 fusion.39
  163.4 1.7 fusion.39
  172.6 1.7 fusion.39
  181.9 1.7 fusion.39
  191.1 1.7 fusion.39
  200.4 1.7 fusion.39
  209.6 1.7 fusion.39
  218.9 1.7 fusion.39
  228.2 1.7 fusion.39
  237.4 1.7 fusion.39
  246.7 1.7 fusion.39
  255.9 1.7 fusion.39
  265.2 1.7 fusion.39
  274.4 1.7 fusion.39
  283.7 1.7 fusion.39
  292.9 1.7 fusion.39
  302.2 1.7 fusion.39
  306.2 15.1 %all-to-all-start = ((bf16[8,448,128]{2,1,0:T(8,128)(2,1)}), bf16[8,448,128]{2,1,0:T(8,128)(2,1)S(1)}, u32[]{:S(2)}, u32[]{:S(2)}) async-start(bf16[8,448,128]{2,1,0:T(8,128)(2,1)} %bitcast.11), calls=%async_computation | async-start | bytes 1835008 | tf_op jit(solution)/shard_map/all_to_all | solution.py:110
  321.3 51.3 %all-to-all-done = bf16[8,448,128]{2,1,0:T(8,128)(2,1)S(1)} async-done(((bf16[8,448,128]{2,1,0:T(8,128)(2,1)}), bf16[8,448,128]{2,1,0:T(8,128)(2,1)S(1)}, u32[]{:S(2)}, u32[]{:S(2)}) %all-to-all-start) | async-done | bytes 917536 | tf_op jit(solution)/shard_map/all_to_all | solution.py:110
  372.5 3.2 add_convert_fusion
  (228 shorter events, 115.0 us)
Async XLA Ops:
  0.0 372.5 %copy-start = (bf16[1024,1024]{1,0:T(8,128)(2,1)S(1)}, bf16[1024,1024]{1,0:T(8,128)(2,1)}, u32[]{:S(2)}) copy-start(bf16[1024,1024]{1,0:T(8,128)(2,1)} %param.13) | copy-start | bytes 6291460
  0.0 5.3 %copy-start.1 = (bf16[3584,1024]{1,0:T(8,128)(2,1)S(1)}, bf16[3584,1024]{1,0:T(8,128)(2,1)}, u32[]{:S(2)}) copy-start(bf16[3584,1024]{1,0:T(8,128)(2,1)} %param.9) | copy-start | bytes 22020100
  5.3 3.5 copy-start.6
  8.9 5.4 %copy-start.5 = (bf16[1024,3,128]{0,2,1:T(8,128)(2,1)}, bf16[1024,3,128]{0,2,1:T(8,128)(2,1)S(1)}, u32[]{:S(2)}) copy-start(bf16[1024,3,128]{0,2,1:T(8,128)(2,1)S(1)} %copy.8) | copy-start | bytes 2359300
  14.2 2.9 copy-start.2
  14.2 5.0 %copy-start.7 = (f32[2,2,64]{2,1,0:T(2,128)S(1)}, f32[2,2,64]{2,1,0:T(2,128)}, u32[]{:S(2)}) copy-start(f32[2,2,64]{2,1,0:T(2,128)} %param.12) | copy-start | bytes 3076
  17.2 1.9 copy-start.4
  21.1 3.6 copy-start.3
  22.3 14.4 %collective-permute-start.1 = (bf16[896,256]{0,1:T(8,128)(2,1)}, bf16[896,256]{0,1:T(8,128)(2,1)S(1)}, u32[]{:S(2)}, u32[]{:S(2)}) collective-permute-start(bf16[896,256]{0,1:T(8,128)(2,1)} %get-tuple-element.92), channel_id=1, source_target_pairs={{32,0},{64,32},{96,64},{128,96},{160,128},{192,160},{224,192},{256... | collective-permute-start | bytes 1376264 | tf_op jit(solution)/shard_map/ppermute | solution.py:20
  24.7 10.5 %copy-start.8 = (s32[28]{0:T(128)S(1)}, s32[28]{0:T(128)}, u32[]{:S(2)}) copy-start(s32[28]{0:T(128)} %param.14) | copy-start | bytes 340
  24.7 14.2 %collective-permute-start = (bf16[896,256]{0,1:T(8,128)(2,1)}, bf16[896,256]{0,1:T(8,128)(2,1)}, u32[]{:S(2)}, u32[]{:S(2)}) collective-permute-start(bf16[896,256]{0,1:T(8,128)(2,1)} %get-tuple-element.91), channel_id=1, source_target_pairs={{0,32},{32,64},{64,96},{96,128},{128,160},{160,192},{192,224},{224... | collective-permute-start | bytes 1376264 | tf_op jit(solution)/shard_map/ppermute | solution.py:18
  45.0 2.1 copy-start.9
  306.2 66.4 %all-to-all-start = ((bf16[8,448,128]{2,1,0:T(8,128)(2,1)}), bf16[8,448,128]{2,1,0:T(8,128)(2,1)S(1)}, u32[]{:S(2)}, u32[]{:S(2)}) async-start(bf16[8,448,128]{2,1,0:T(8,128)(2,1)} %bitcast.11), calls=%async_computation | async-start | bytes 1835008 | tf_op jit(solution)/shard_map/all_to_all | solution.py:110
where the time goes:
time: 379 us; the launch traced here: 376 us
  matrix products  101 us (27%)
  loops' own time  97.5 us (26%)
  local copies, waits for them, and re-layouts  78.5 us (21%)
  waiting for transfers between devices  55 us (15%)
  other arithmetic  22.2 us (6%)
  starting transfers between devices  21.1 us (6%)
    another operation x1, loops' own time, attend(): result = lax.map(one_block, jnp.arange(num_blocks, dtype=jnp.int32))  97.5 us
    all_to_all x1, waiting for transfers between devices, on_device(): lax.all_to_all(attended, 'head', split_axis=0, concat_axis=1, tiled=True)  51.3 us
    dot_general x28, matrix products, one_block(): jnp.einsum('hid,hjd->hij', query_block, key_window, preferred_element_typ...  48 us
    dot_general x28, matrix products, one_block(): jnp.einsum('hij,hjd->hid', weights.astype(jnp.bfloat16), value_window, pr...  42.2 us
    dynamic_update_slice x56, local copies, waits for them, and re-layouts, attend(): result = lax.map(one_block, jnp.arange(num_blocks, dtype=jnp.int32))  20.8 us
    dynamic_slice x28, local copies, waits for them, and re-layouts, one_block(): first_row = local_first[block_index] * BLOCK  17.9 us
    dynamic_slice x28, local copies, waits for them, and re-layouts, one_block(): live = positions < counts[block_index] * BLOCK  16.4 us
    dynamic_slice x28, local copies, waits for them, and re-layouts, attend(): result = lax.map(one_block, jnp.arange(num_blocks, dtype=jnp.int32))  16.2 us
  transfers between devices with their start and end apart: 3, of which 3 were waited for; matrix products, arithmetic and copies ran while one was open for 2% of the time, Pallas kernels for 0%

commit v1 on v0

v1 whole, which is shorter than its diff:
```python
import functools

import jax
import jax.numpy as jnp
from jax import lax
from jax.experimental import pallas as pl
from jax.experimental.pallas import tpu as pltpu
from jax.sharding import PartitionSpec as P

BLOCK = 128
REACH = 7
SPAN = (2 * REACH + 1) * BLOCK
CHUNK = 256
LOG2E = 1.4426950408889634
DEAD = -30000.0
F32 = jnp.float32
BF16 = jnp.bfloat16


def pair_ones():
    row = lax.broadcasted_iota(jnp.int32, (256, 128), 0)
    col = lax.broadcasted_iota(jnp.int32, (256, 128), 1)
    return (((row // 64) % 2) == (col // 64)).astype(BF16)


def layer_normed(values, gain):
    center = jnp.mean(values, axis=-1, keepdims=True)
    shifted = values - center
    spread = jnp.mean(jnp.square(shifted), axis=-1, keepdims=True)
    return (shifted * lax.rsqrt(spread + 1e-05) * gain).astype(BF16)


def head_normed(raw, gain, ones):
    square = raw * raw
    high = square.astype(BF16)
    low = (square - high.astype(F32)).astype(BF16)
    total = jnp.dot(jnp.concatenate([high, low], 1), ones, preferred_element_type=F32)
    return (raw * lax.rsqrt(total * (1.0 / 64.0) + 1e-06) * gain).astype(BF16)


def project(tok_ref, ln_ref, w_ref, gain_ref, q_ref, kv_ref):
    normed = layer_normed(tok_ref[...].astype(F32), ln_ref[...])
    raw = jnp.dot(normed, w_ref[...], preferred_element_type=F32)
    ones = pair_ones()
    q_ref[...] = head_normed(raw[:, :128], gain_ref[0:1, :] * (LOG2E / 8.0), ones)
    kv_ref[:, :128] = head_normed(raw[:, 128:256], gain_ref[1:2, :], ones)
    kv_ref[:, 128:] = raw[:, 256:].astype(BF16)


def attend(q_ref, left_ref, mid_ref, right_ref, bias_ref, out_ref, ka, va):
    width = REACH * BLOCK
    rows = mid_ref.shape[0]
    for ref, first, count in ((left_ref, 0, width), (mid_ref, width, rows), (right_ref, width + rows, width)):
        ka[pl.ds(first, count), :128] = ref[:, :128]
        va[pl.ds(first, count), :128] = ref[:, 128:]
    total = rows + 2 * width
    block_id = lax.broadcasted_iota(jnp.int32, (total, 128), 0) // BLOCK
    ka[:, 128:] = (block_id == lax.broadcasted_iota(jnp.int32, (total, 128), 1)).astype(BF16)
    va[:, 128:] = jnp.ones((total, 128), BF16)
    lane = lax.broadcasted_iota(jnp.int32, (BLOCK, 128), 1)

    def one_block(i, carry):
        first = pl.multiple_of(i * BLOCK, BLOCK)
        q = q_ref[pl.ds(first, BLOCK), :]
        zero = jnp.zeros_like(q)
        bias = jnp.broadcast_to(bias_ref[pl.ds(i, 1), :], (BLOCK, 128)).astype(BF16)
        both = jnp.concatenate(
            [
                jnp.concatenate([jnp.where(lane < 64, q, zero), bias], 1),
                jnp.concatenate([jnp.where(lane < 64, zero, q), bias], 1),
            ],
            0,
        )
        acc = None
        for j in range(0, SPAN, CHUNK):
            count = min(CHUNK, SPAN - j)
            scores = lax.dot_general(
                both, ka[pl.ds(first + j, count), :], (((1,), (1,)), ((), ())), preferred_element_type=F32
            )
            weights = jnp.exp2(scores).astype(BF16)
            part = jnp.dot(weights, va[pl.ds(first + j, count), :], preferred_element_type=F32)
            acc = part if acc is None else acc + part
        mixed = acc[:, :128] * (1.0 / acc[:, 128:])
        out_ref[pl.ds(first, BLOCK), :] = jnp.where(lane < 64, mixed[:BLOCK], mixed[BLOCK:]).astype(BF16)
        return carry

    lax.fori_loop(0, rows // BLOCK, one_block, 0)


def on_device(tokens, ln_gain, qkv_weight, qk_gain, out_weight, key_start, key_count):
    rows, features = tokens.shape
    columns = qk_gain.shape[1] * qk_gain.shape[2]
    num_blocks = rows // BLOCK
    width = REACH * BLOCK
    step = 448
    weight = qkv_weight.reshape(features, 3 * columns)
    whole = pl.BlockSpec(memory_space=pltpu.VMEM)
    queries, kv = pl.pallas_call(
        project,
        grid=(rows // step,),
        out_shape=(
            jax.ShapeDtypeStruct((rows, columns), BF16),
            jax.ShapeDtypeStruct((rows, 2 * columns), BF16),
        ),
        in_specs=[pl.BlockSpec((step, features), lambda i: (i, 0)), whole, whole, whole],
        out_specs=(
            pl.BlockSpec((step, columns), lambda i: (i, 0)),
            pl.BlockSpec((step, 2 * columns), lambda i: (i, 0)),
        ),
        compiler_params=pltpu.CompilerParams(vmem_limit_bytes=40 << 20),
        name="project",
    )(tokens, ln_gain.reshape(1, features), weight, qk_gain.reshape(2, columns))
    band = lax.axis_size("band")
    left = lax.ppermute(kv[rows - width :], "band", [(i, i + 1) for i in range(band - 1)])
    right = lax.ppermute(kv[:width], "band", [(i + 1, i) for i in range(band - 1)])
    first = (key_start - (lax.axis_index("band") * num_blocks - REACH))[:, None]
    block = jnp.arange(128, dtype=jnp.int32)[None, :]
    live = (block >= first) & (block < first + key_count[:, None])
    bias = jnp.where(live, 0.0, DEAD).astype(F32)
    attended = pl.pallas_call(
        attend,
        out_shape=jax.ShapeDtypeStruct((rows, columns), BF16),
        in_specs=[whole] * 5,
        out_specs=whole,
        scratch_shapes=[
            pltpu.VMEM((rows + 2 * width, 256), BF16),
            pltpu.VMEM((rows + 2 * width, 256), BF16),
        ],
        compiler_params=pltpu.CompilerParams(vmem_limit_bytes=40 << 20),
        name="attend",
    )(queries, left, kv, right, bias)
    share = rows // lax.axis_size("head")
    head_pos = lax.axis_index("head")
    residual_rows = lax.dynamic_slice_in_dim(tokens, head_pos * share, share, 0).astype(F32)
    all_heads = lax.all_to_all(attended, "head", split_axis=0, concat_axis=1, tiled=True)
    summed = jnp.dot(all_heads, out_weight, preferred_element_type=F32)
    return (residual_rows + summed).astype(BF16)


def solution(mesh):
    placed = (
        P(("member", "band"), None),
        P(),
        P(None, None, "head"),
        P(None, "head", None),
        P(),
        P("band"),
        P("band"),
    )
    return jax.shard_map(
        on_device,
        mesh=mesh,
        in_specs=placed,
        out_specs=P(("member", "band", "head"), None),
        check_vma=False,
    )
```

time: 379 us -> 140 us (0.37)
  matrix products: 101 us -> 3.22 us
  loops' own time: 97.5 us -> 0 us
  local copies, waits for them, and re-layouts: 78.5 us -> 12.8 us
  Pallas kernels: 0 us -> 41.1 us
  other arithmetic: 22.2 us -> 0.08 us
  waiting for transfers between devices: 55 us -> 61.6 us
    dot_general x59 -> x1, matrix products: 101 us -> 3.22 us  [on_device(): summed = jnp.dot(all_heads, out_weight, preferred_element_type=F32)]
    another operation x1 -> x0, loops' own time: 97.5 us -> none  [attend(): result = lax.map(one_block, jnp.arange(num_blocks, dtype=jnp.int32))]
    dynamic_slice x84 -> x0, local copies, waits for them, and re-layouts: 50.4 us -> none  [the longest x28 17.9 us: one_block(): first_row = local_first[block_index] * BLOCK]
    pallas_call x0 -> x2, Pallas kernels: none -> 41.1 us  [the longest x1 31.7 us: on_device(): pl.pallas_call(attend, out_shape=jax.ShapeDtypeStruct((rows, columns), BF...]
    dynamic_update_slice x56 -> x0, local copies, waits for them, and re-layouts: 20.8 us -> none  [attend(): result = lax.map(one_block, jnp.arange(num_blocks, dtype=jnp.int32))]
    convert_element_type x2 -> x0, other arithmetic: 7.07 us -> none  [the longest x1 5.36 us: layer_normed(): ((values - center) * lax.rsqrt(spread + 1e-05) * ln_gain).astype(jnp.bflo...]
    ppermute x2, waiting for transfers between devices: 3.73 us -> 10.4 us  [the longest x1 8.39 us: on_device(): lax.ppermute(kv[:width], 'band', [(i + 1, i) for i in range(band - 1)])]
    reduce_sum x3 -> x0, other arithmetic: 6.54 us -> none  [the longest x1 4.27 us: layer_normed(): center = jnp.mean(values, axis=-1, keepdims=True)]
  transfers between devices with their start and end apart: 3 -> 3, of which waited for: 3 -> 3; matrix products, arithmetic and copies ran while one was open for 2% -> 0% of each run, Pallas kernels for 0% -> 0%
where the time goes in v1:
time: 140 us
  waiting for transfers between devices  61.6 us (44%)
  Pallas kernels  41.1 us (29%)
  starting transfers between devices  20.9 us (15%)
  local copies, waits for them, and re-layouts  12.8 us (9%)
  matrix products  3.22 us (2%)
    all_to_all x1, waiting for transfers between devices, on_device(): lax.all_to_all(attended, 'head', split_axis=0, concat_axis=1, tiled=True)  51.3 us
    pallas_call x1, Pallas kernels, on_device(): pl.pallas_call(attend, out_shape=jax.ShapeDtypeStruct((rows, columns), BF...  31.7 us
    all_to_all x1, starting transfers between devices, on_device(): lax.all_to_all(attended, 'head', split_axis=0, concat_axis=1, tiled=True)  15.1 us
    unnamed x19, local copies, waits for them, and re-layouts  9.48 us
    pallas_call x1, Pallas kernels, on_device(): pl.pallas_call(project, grid=(rows // step,), out_shape=(jax.ShapeDtypeSt...  9.43 us
    ppermute x1, waiting for transfers between devices, on_device(): lax.ppermute(kv[:width], 'band', [(i + 1, i) for i in range(band - 1)])  8.39 us
    ppermute x1, starting transfers between devices, on_device(): lax.ppermute(kv[rows - width:], 'band', [(i, i + 1) for i in range(band -...  3.4 us
    dot_general x1, matrix products, on_device(): summed = jnp.dot(all_heads, out_weight, preferred_element_type=F32)  3.22 us
  transfers between devices with their start and end apart: 3, of which 3 were waited for; matrix products, arithmetic and copies ran while one was open for 0% of the time, Pallas kernels for 0%

profile of v1, /device:TPU:10, one launch (start us, length us, event | category | flops | bytes accessed | tf_op | source)
XLA Modules:
  0.0 139.8 jit_solution(13938589048358380550)
XLA Ops:
  0.0 0.0 copy-start
  0.0 0.0 copy-start.6
  0.0 0.9 reshape.17.gain_ref
  0.9 2.3 %copy.12 = bf16[1024,3,128]{0,2,1:T(8,128)(2,1)} copy(bf16[1024,3,128]{2,0,1:T(8,128)(2,1)} %param.9) | data formatting | bytes 1572864 | tf_op args[2]
  3.2 1.5 %copy.13.w_ref = bf16[1024,384]{1,0:T(8,128)(2,1)S(1)} copy(bf16[1024,384]{0,1:T(8,128)(2,1)} %bitcast.13) | data formatting | bytes 1572864 | tf_op jit(solution)/shard_map/reshape | solution.py:96
  4.7 0.0 copy-done.6
  4.7 0.0 copy-start.1
  4.7 3.1 %copy-done.1 = bf16[3584,1024]{1,0:T(8,128)(2,1)S(1)} copy-done((bf16[3584,1024]{1,0:T(8,128)(2,1)S(1)}, bf16[3584,1024]{1,0:T(8,128)(2,1)}, u32[]{:S(2)}) %copy-start.1) | copy-done | bytes 7340056
  7.8 0.0 copy-start.7
  7.8 0.0 copy-start.8
  7.8 9.4 %project.1 = (bf16[3584,128]{1,0:T(8,128)(2,1)S(1)}, bf16[3584,256]{1,0:T(8,128)(2,1)S(1)}) custom-call(bf16[3584,1024]{1,0:T(8,128)(2,1)S(1)} %copy-done.1, f32[1,1024]{1,0:T(1,128)S(1)} %bitcast.12, bf16[1024,384]{1,0:T(8,128)(2,1)S(1)} %copy.13.w_ref, f32[2,128]{1,0:T(2,128)S(1)} %reshape.17.gain_ref), custom_call_target="tpu_custom_call" | custom-call | tf_op jit(solution)/shard_map/project/pallas_call | solution.py:98
  17.2 0.0 copy-start.4
  17.3 0.9 fusion.5
  18.2 0.1 copy-done.4
  18.3 0.0 copy-start.2
  18.3 1.3 copy-done.2
  19.6 2.4 %collective-permute-start.1 = (bf16[896,256]{1,0:T(8,128)(2,1)}, bf16[896,256]{1,0:T(8,128)(2,1)S(1)}, u32[]{:S(2)}, u32[]{:S(2)}) collective-permute-start(bf16[896,256]{1,0:T(8,128)(2,1)} %get-tuple-element.11), channel_id=1, source_target_pairs={{32,0},{64,32},{96,64},{128,96},{160,128},{192,160},{224,192},{256... | collective-permute-start | bytes 1376264 | tf_op jit(solution)/shard_map/ppermute | solution.py:115
  22.0 3.4 %collective-permute-start = (bf16[896,256]{1,0:T(8,128)(2,1)S(1)}, bf16[896,256]{1,0:T(8,128)(2,1)S(1)}, u32[]{:S(2)}, u32[]{:S(2)}) collective-permute-start(bf16[896,256]{1,0:T(8,128)(2,1)S(1)} %get-tuple-element.12), channel_id=1, source_target_pairs={{0,32},{32,64},{64,96},{96,128},{128,160},{160,192},{192,224},{224... | collective-permute-start | bytes 1376264 | tf_op jit(solution)/shard_map/ppermute | solution.py:114
  25.4 0.0 copy-done.7
  25.5 0.0 copy-done.8
  25.5 0.1 fusion.3.bias_ref
  25.6 8.4 %collective-permute-done.1.right_ref = bf16[896,256]{1,0:T(8,128)(2,1)S(1)} collective-permute-done((bf16[896,256]{1,0:T(8,128)(2,1)}, bf16[896,256]{1,0:T(8,128)(2,1)S(1)}, u32[]{:S(2)}, u32[]{:S(2)}) %collective-permute-start.1) | collective-permute-done | bytes 458784 | tf_op jit(solution)/shard_map/ppermute | solution.py:115
  33.9 2.0 %collective-permute-done.left_ref = bf16[896,256]{1,0:T(8,128)(2,1)S(1)} collective-permute-done((bf16[896,256]{1,0:T(8,128)(2,1)S(1)}, bf16[896,256]{1,0:T(8,128)(2,1)S(1)}, u32[]{:S(2)}, u32[]{:S(2)}) %collective-permute-start) | collective-permute-done | bytes 458784 | tf_op jit(solution)/shard_map/ppermute | solution.py:114
  35.9 0.0 copy-start.3
  35.9 1.5 %copy-done.3 = bf16[3584,256]{1,0:T(8,128)(2,1)S(1)} copy-done((bf16[3584,256]{1,0:T(8,128)(2,1)S(1)}, bf16[3584,256]{1,0:T(8,128)(2,1)}, u32[]{:S(2)}) %copy-start.3) | copy-done | bytes 1835032
  37.4 0.0 copy-start.5
  37.4 1.2 copy-done.5
  38.6 31.7 %attend.1 = bf16[3584,128]{1,0:T(8,128)(2,1)} custom-call(bf16[3584,128]{1,0:T(8,128)(2,1)S(1)} %copy-done.5, bf16[896,256]{1,0:T(8,128)(2,1)S(1)} %collective-permute-done.left_ref, bf16[3584,256]{1,0:T(8,128)(2,1)S(1)} %copy-done.3, bf16[896,256]{1,0:T(8,128)(2,1)S(1)} %collective-permute-done.1.right_ref, f32[28,128]{1,0:T(8,128)S(1)} %fusion.3.bias_ref), custom_call_target="tpu_custom_call" | custom-call | tf_op jit(solution)/shard_map/attend/pallas_call | solution.py:120
  70.3 15.1 %all-to-all-start = ((bf16[8,448,128]{2,1,0:T(8,128)(2,1)}), bf16[8,448,128]{2,1,0:T(8,128)(2,1)S(1)}, u32[]{:S(2)}, u32[]{:S(2)}) async-start(bf16[8,448,128]{2,1,0:T(8,128)(2,1)} %bitcast.2), calls=%async_computation | async-start | bytes 1835008 | tf_op jit(solution)/shard_map/all_to_all | solution.py:135
  85.3 51.3 %all-to-all-done = bf16[8,448,128]{2,1,0:T(8,128)(2,1)S(1)} async-done(((bf16[8,448,128]{2,1,0:T(8,128)(2,1)}), bf16[8,448,128]{2,1,0:T(8,128)(2,1)S(1)}, u32[]{:S(2)}, u32[]{:S(2)}) %all-to-all-start) | async-done | bytes 917536 | tf_op jit(solution)/shard_map/all_to_all | solution.py:135
  136.6 0.0 copy-done
  136.6 3.2 %add_convert_fusion = bf16[448,1024]{1,0:T(8,128)(2,1)} fusion(bf16[1024,1024]{1,0:T(8,128)(2,1)S(1)} %copy-done, bf16[3584,1024]{1,0:T(8,128)(2,1)} %tok_ref.1, s32[]{:T(128)S(6)} %select_n.7, bf16[8,448,128]{2,1,0:T(8,128)(2,1)S(1)} %all-to-all-done), kind=kOutput, calls=%fused_computation | convolution fusion | flops 940900352 | bytes 4849668 | tf_op jit(solution)/shard_map/dot_general | solution.py:136
  (1 shorter events, 0.0 us)
Async XLA Ops:
  0.0 136.6 %copy-start = (bf16[1024,1024]{1,0:T(8,128)(2,1)S(1)}, bf16[1024,1024]{1,0:T(8,128)(2,1)}, u32[]{:S(2)}) copy-start(bf16[1024,1024]{1,0:T(8,128)(2,1)} %param.11) | copy-start | bytes 6291460
  0.0 4.7 %copy-start.6 = (f32[1024]{0:T(1024)S(1)}, f32[1024]{0:T(1024)}, u32[]{:S(2)}) copy-start(f32[1024]{0:T(1024)} %param.8) | copy-start | bytes 12292
  4.7 3.1 %copy-start.1 = (bf16[3584,1024]{1,0:T(8,128)(2,1)S(1)}, bf16[3584,1024]{1,0:T(8,128)(2,1)}, u32[]{:S(2)}) copy-start(bf16[3584,1024]{1,0:T(8,128)(2,1)} %tok_ref.1) | copy-start | bytes 22020100
  7.8 17.6 %copy-start.7 = (s32[28]{0:T(128)S(1)}, s32[28]{0:T(128)}, u32[]{:S(2)}) copy-start(s32[28]{0:T(128)} %param.13) | copy-start | bytes 340
  7.8 17.7 %copy-start.8 = (s32[28]{0:T(128)S(1)}, s32[28]{0:T(128)}, u32[]{:S(2)}) copy-start(s32[28]{0:T(128)} %param.12) | copy-start | bytes 340
  17.2 1.1 copy-start.4
  18.3 1.3 copy-start.2
  19.6 14.4 %collective-permute-start.1 = (bf16[896,256]{1,0:T(8,128)(2,1)}, bf16[896,256]{1,0:T(8,128)(2,1)S(1)}, u32[]{:S(2)}, u32[]{:S(2)}) collective-permute-start(bf16[896,256]{1,0:T(8,128)(2,1)} %get-tuple-element.11), channel_id=1, source_target_pairs={{32,0},{64,32},{96,64},{128,96},{160,128},{192,160},{224,192},{256... | collective-permute-start | bytes 1376264 | tf_op jit(solution)/shard_map/ppermute | solution.py:115
  22.0 13.9 %collective-permute-start = (bf16[896,256]{1,0:T(8,128)(2,1)S(1)}, bf16[896,256]{1,0:T(8,128)(2,1)S(1)}, u32[]{:S(2)}, u32[]{:S(2)}) collective-permute-start(bf16[896,256]{1,0:T(8,128)(2,1)S(1)} %get-tuple-element.12), channel_id=1, source_target_pairs={{0,32},{32,64},{64,96},{96,128},{128,160},{160,192},{192,224},{224... | collective-permute-start | bytes 1376264 | tf_op jit(solution)/shard_map/ppermute | solution.py:114
  35.9 1.5 %copy-start.3 = (bf16[3584,256]{1,0:T(8,128)(2,1)S(1)}, bf16[3584,256]{1,0:T(8,128)(2,1)}, u32[]{:S(2)}) copy-start(bf16[3584,256]{1,0:T(8,128)(2,1)} %copy-done.2) | copy-start | bytes 5505028
  37.4 1.2 copy-start.5
  70.3 66.4 %all-to-all-start = ((bf16[8,448,128]{2,1,0:T(8,128)(2,1)}), bf16[8,448,128]{2,1,0:T(8,128)(2,1)S(1)}, u32[]{:S(2)}, u32[]{:S(2)}) async-start(bf16[8,448,128]{2,1,0:T(8,128)(2,1)} %bitcast.2), calls=%async_computation | async-start | bytes 1835008 | tf_op jit(solution)/shard_map/all_to_all | solution.py:135

commit v2 on v1

v2 whole, which is shorter than its diff:
```python
import jax
import jax.numpy as jnp
from jax import lax
from jax.experimental import pallas as pl
from jax.experimental.pallas import tpu as pltpu
from jax.sharding import PartitionSpec as P

BLOCK = 128
REACH = 7
WIDE = REACH * BLOCK
SPAN = (2 * REACH + 1) * BLOCK
HALF = WIDE // 2
STEP = 448
CHUNK = 256
LOG2E = 1.4426950408889634
DEAD = -30000.0
F32 = jnp.float32
BF16 = jnp.bfloat16
MESH = pl.DeviceIdType.MESH


def pair_ones():
    row = lax.broadcasted_iota(jnp.int32, (256, 128), 0)
    col = lax.broadcasted_iota(jnp.int32, (256, 128), 1)
    return (((row // 64) % 2) == (col // 64)).astype(BF16)


def layer_normed(values, gain):
    center = jnp.mean(values, axis=-1, keepdims=True)
    shifted = values - center
    spread = jnp.mean(jnp.square(shifted), axis=-1, keepdims=True)
    return (shifted * lax.rsqrt(spread + 1e-05) * gain).astype(BF16)


def head_normed(raw, gain, ones):
    square = raw * raw
    high = square.astype(BF16)
    low = (square - high.astype(F32)).astype(BF16)
    total = jnp.dot(jnp.concatenate([high, low], 1), ones, preferred_element_type=F32)
    return (raw * lax.rsqrt(total * (1.0 / 64.0) + 1e-06) * gain).astype(BF16)


def rows_at(first, count):
    return pl.ds(pl.multiple_of(first, 64), count)


def attend_block(q, bias, kv, first, lane):
    zero = jnp.zeros_like(q)
    bias = jnp.broadcast_to(bias, (BLOCK, 128)).astype(BF16)
    both = jnp.concatenate(
        [
            jnp.concatenate([jnp.where(lane < 64, q, zero), bias], 1),
            jnp.concatenate([jnp.where(lane < 64, zero, q), bias], 1),
        ],
        0,
    )
    acc = None
    for j in range(0, SPAN, CHUNK):
        count = min(CHUNK, SPAN - j)
        marks = [(lane == (j // BLOCK + m)).astype(BF16) for m in range(count // BLOCK)]
        keys = jnp.concatenate([kv[rows_at(first + j, count), :128], jnp.concatenate(marks, 0)], 1)
        values = jnp.concatenate([kv[rows_at(first + j, count), 128:], jnp.ones((count, 128), BF16)], 1)
        scores = lax.dot_general(both, keys, (((1,), (1,)), ((), ())), preferred_element_type=F32)
        part = jnp.dot(jnp.exp2(scores).astype(BF16), values, preferred_element_type=F32)
        acc = part if acc is None else acc + part
    mixed = acc[:, :128] * (1.0 / acc[:, 128:])
    return jnp.where(lane < 64, mixed[:BLOCK], mixed[BLOCK:]).astype(BF16)


def layer(
    tok, ln, w_hbm, gain, ow_hbm, bias, out,
    xv, w, ow, kv, qs, att, rcv, res,
    in_sem, w_sem, halo_send, halo_recv, give_send, give_recv, keep_sem,
):
    band = lax.axis_index("band")
    head = lax.axis_index("head")
    bands = 16
    t = head // 2
    c = head % 2
    t_op = (t + 2) % 4
    t_a = 1 + t % 2
    t_b = 3 * ((t + 1) % 2)

    order = (3, 0, 1, 2)
    loads = {}
    for ch in order:
        loads[ch] = pltpu.make_async_copy(
            tok.at[pl.ds(ch * WIDE, WIDE), :], xv.at[pl.ds(ch * WIDE, WIDE), :], in_sem.at[ch]
        )
    loads[3].start()
    load_w = pltpu.make_async_copy(w_hbm, w, w_sem.at[0])
    load_w.start()
    for ch in order[1:]:
        loads[ch].start()
    load_ow = pltpu.make_async_copy(ow_hbm, ow, w_sem.at[1])
    load_ow.start()
    load_res = pltpu.make_async_copy(tok.at[rows_at(t * WIDE + c * HALF, HALF), :], res, w_sem.at[2])
    load_res.start()

    barrier = pltpu.get_barrier_semaphore()
    for d in range(1, 8):
        pl.semaphore_signal(barrier, inc=1, device_id={"head": (head + d) % 8}, device_id_type=MESH)

    for d in (1, bands - 1):
        pl.semaphore_signal(barrier, inc=1, device_id={"band": (band + d) % bands}, device_id_type=MESH)

    @pl.when(band == 0)
    def _():
        kv[pl.ds(0, WIDE), :] = jnp.zeros((WIDE, 256), BF16)

    @pl.when(band == bands - 1)
    def _():
        kv[pl.ds(5 * WIDE, WIDE), :] = jnp.zeros((WIDE, 256), BF16)

    ones = pair_ones()
    q_gain = gain[0:1, :] * (LOG2E / 8.0)
    k_gain = gain[1:2, :]

    def project(ch):
        def step(s, carry):
            first = ch * WIDE + s * STEP
            normed = layer_normed(xv[rows_at(first, STEP), :].astype(F32), ln[...])
            raw = jnp.dot(normed, w[...], preferred_element_type=F32)
            qs[rows_at(first, STEP), :] = head_normed(raw[:, :128], q_gain, ones)
            kv[rows_at(WIDE + first, STEP), :128] = head_normed(raw[:, 128:256], k_gain, ones)
            kv[rows_at(WIDE + first, STEP), 128:] = raw[:, 256:].astype(BF16)
            return carry

        lax.fori_loop(0, WIDE // STEP, step, 0)

    def halo(side):
        return pltpu.make_async_remote_copy(
            src_ref=kv.at[pl.ds((4 - 3 * side) * WIDE, WIDE), :],
            dst_ref=kv.at[pl.ds(5 * side * WIDE, WIDE), :],
            send_sem=halo_send.at[side],
            recv_sem=halo_recv.at[side],
            device_id={"band": band + 1 - 2 * side},
            device_id_type=MESH,
        )

    loads[3].wait()
    load_w.wait()
    project(3)
    pl.semaphore_wait(barrier, 9)

    @pl.when(band < bands - 1)
    def _():
        halo(0).start()

    loads[0].wait()
    project(0)

    @pl.when(band > 0)
    def _():
        halo(1).start()

    for ch in (1, 2):
        loads[ch].wait()
        project(ch)

    lane = lax.broadcasted_iota(jnp.int32, (BLOCK, 128), 1)
    column = pl.multiple_of(head * 128, 128)

    def give(unit, part, chip, core, slot):
        return pltpu.make_async_remote_copy(
            src_ref=att.at[pl.ds(unit * WIDE + part * HALF, HALF), :],
            dst_ref=rcv.at[:, pl.ds(column, 128)],
            send_sem=give_send.at[slot],
            recv_sem=give_recv.at[head],
            device_id={"head": chip * 2 + core},
            device_id_type=MESH,
        )

    chips = (t_a, t_op, t_b, t)

    def block(unit, i):
        first = chips[unit] * WIDE + i * BLOCK
        att[pl.ds(unit * WIDE + i * BLOCK, BLOCK), :] = attend_block(
            qs[rows_at(first, BLOCK), :], bias[pl.ds(chips[unit] * REACH + i, 1), :], kv, first, lane
        )

    for i in range(7):
        block(0, i)
        if i == 3:
            give(0, 0, t_a, 0, 0).start()
    give(0, 1, t_a, 1, 1).start()

    @pl.when(band > 0)
    def _():
        halo(0).wait_recv()

    @pl.when(band < bands - 1)
    def _():
        halo(1).wait_recv()

    for part in range(2):
        for unit in (1, 2):
            for i in range(4 * part, 4 + 3 * part):
                block(unit, i)
            give(unit, part, chips[unit], part, 2 * unit + part).start()
    for i in range(7):
        block(3, i)
        if i == 3:

            @pl.when(c == 1)
            def _():
                give(3, 0, t, 0, 6).start()

    keep = pltpu.make_async_copy(
        att.at[pl.ds(pl.multiple_of(3 * WIDE + c * HALF, 64), HALF), :], rcv.at[:, pl.ds(column, 128)], keep_sem
    )
    keep.start()

    @pl.when(c == 0)
    def _():
        give(3, 1, t, 1, 6).start()

    load_ow.wait()
    load_res.wait()
    keep.wait()
    for d in range(1, 8):
        peer = (head + d) % 8
        pltpu.make_async_remote_copy(
            src_ref=att.at[pl.ds(0, HALF), :],
            dst_ref=rcv.at[:, pl.ds(pl.multiple_of(peer * 128, 128), 128)],
            send_sem=give_send.at[0],
            recv_sem=give_recv.at[peer],
            device_id={"head": peer},
            device_id_type=MESH,
        ).wait_recv()
    for r in range(0, HALF, 224):
        summed = jnp.dot(rcv[pl.ds(r, 224), :], ow[...], preferred_element_type=F32)
        out[pl.ds(r, 224), :] = (res[pl.ds(r, 224), :].astype(F32) + summed).astype(BF16)
    for slot, unit in enumerate((0, 0, 1, 1, 2, 2)):
        give(unit, slot % 2, chips[unit], slot % 2, slot).wait_send()

    @pl.when(c == 1)
    def _():
        give(3, 0, t, 0, 6).wait_send()

    @pl.when(c == 0)
    def _():
        give(3, 1, t, 1, 6).wait_send()

    @pl.when(band < bands - 1)
    def _():
        halo(0).wait_send()

    @pl.when(band > 0)
    def _():
        halo(1).wait_send()


def on_device(tokens, ln_gain, qkv_weight, qk_gain, out_weight, key_start, key_count):
    rows, features = tokens.shape
    columns = qk_gain.shape[1] * qk_gain.shape[2]
    num_blocks = rows // BLOCK
    weight = qkv_weight.reshape(features, 3 * columns)
    ids = lax.axis_index("band") * num_blocks + jnp.arange(num_blocks, dtype=jnp.int32)
    first = (key_start - (ids - REACH))[:, None]
    block = jnp.arange(128, dtype=jnp.int32)[None, :]
    live = (block >= first) & (block < first + key_count[:, None])
    bias = jnp.where(live, 0.0, DEAD).astype(F32)
    whole = pl.BlockSpec(memory_space=pltpu.VMEM)
    far = pl.BlockSpec(memory_space=pl.ANY)
    return pl.pallas_call(
        layer,
        out_shape=jax.ShapeDtypeStruct((HALF, features), BF16),
        in_specs=[far, whole, far, whole, far, whole],
        out_specs=whole,
        scratch_shapes=[
            pltpu.VMEM((rows, features), BF16),
            pltpu.VMEM((features, 3 * columns), BF16),
            pltpu.VMEM((features, features), BF16),
            pltpu.VMEM((6 * WIDE, 256), BF16),
            pltpu.VMEM((rows, 128), BF16),
            pltpu.VMEM((rows, 128), BF16),
            pltpu.VMEM((HALF, features), BF16),
            pltpu.VMEM((HALF, features), BF16),
            pltpu.SemaphoreType.DMA((4,)),
            pltpu.SemaphoreType.DMA((3,)),
            pltpu.SemaphoreType.DMA((2,)),
            pltpu.SemaphoreType.DMA((2,)),
            pltpu.SemaphoreType.DMA((7,)),
            pltpu.SemaphoreType.DMA((8,)),
            pltpu.SemaphoreType.DMA,
        ],
        compiler_params=pltpu.CompilerParams(
            vmem_limit_bytes=56 << 20, collective_id=0, has_side_effects=True
        ),
        name="layer",
    )(tokens, ln_gain.reshape(1, features), weight, qk_gain.reshape(2, columns), out_weight, bias)


def solution(mesh):
    placed = (
        P(("member", "band"), None),
        P(),
        P(None, None, "head"),
        P(None, "head", None),
        P(),
        P("band"),
        P("band"),
    )
    return jax.shard_map(
        on_device,
        mesh=mesh,
        in_specs=placed,
        out_specs=P(("member", "band", "head"), None),
        check_vma=False,
    )
```

time: 140 us -> 86.2 us (0.62)
  the two profiles are of different devices: /device:TPU:10 before, /device:TPU:1 now
where the time goes in v2:
time: 86.2 us; the launch traced here: 86 us
  Pallas kernels  78.5 us (91%)
  local copies, waits for them, and re-layouts  6.05 us (7%)
  other arithmetic  1.35 us (2%)
    pallas_call x1, Pallas kernels, on_device(): pl.pallas_call(layer, out_shape=jax.ShapeDtypeStruct((HALF, features), BF...  78.5 us
    unnamed x2, local copies, waits for them, and re-layouts  3.56 us

profile of v2, /device:TPU:1, one launch (start us, length us, event | category | flops | bytes accessed | tf_op | source)
XLA Modules:
  0.0 86.0 jit_solution(12582819092789972751)
XLA Ops:
  0.0 0.7 fusion.2
  0.7 1.3 %reshape.14.gain = f32[2,128]{1,0:T(2,128)} reshape(f32[2,2,64]{2,1,0:T(2,128)} %param.10) | data formatting | bytes 2048 | tf_op jit(solution)/shard_map/reshape | solution.py:292
  2.0 0.7 fusion.1.bias
  2.7 1.4 %copy.9 = bf16[1024,3,128]{0,2,1:T(8,128)(2,1)S(1)} copy(bf16[1024,3,128]{2,0,1:T(8,128)(2,1)} %param.9) | data formatting | bytes 1572864 | tf_op args[2]
  4.1 1.2 %copy.10.w_hbm = bf16[1024,384]{1,0:T(8,128)(2,1)} copy(bf16[1024,384]{0,1:T(8,128)(2,1)S(1)} %bitcast.2) | data formatting | bytes 1572864 | tf_op jit(solution)/shard_map/reshape | solution.py:258
  5.3 78.5 %layer.1 = bf16[448,1024]{1,0:T(8,128)(2,1)} custom-call(bf16[3584,1024]{1,0:T(8,128)(2,1)} %tok.1, f32[1,1024]{1,0:T(1,128)} %bitcast.3, bf16[1024,384]{1,0:T(8,128)(2,1)} %copy.10.w_hbm, f32[2,128]{1,0:T(2,128)} %reshape.14.gain, bf16[1024,1024]{1,0:T(8,128)(2,1)} %ow_hbm.1, f32[28,128]{1,0:T(8,128)} %fusion.1.bias), custom_call_target="tpu_custom_call" | custom-call | tf_op jit(solution)/shard_map/layer/pallas_call | solution.py:266
  83.8 2.2 %copy.12 = bf16[448,1024]{1,0:T(8,128)(2,1)} copy(bf16[448,1024]{1,0:T(8,128)(2,1)} %layer.1) | data formatting | bytes 1835008

commit v3 on v2

v3 whole, which is shorter than its diff:
```python
import jax
import jax.numpy as jnp
from jax import lax
from jax.experimental import pallas as pl
from jax.experimental.pallas import tpu as pltpu
from jax.sharding import PartitionSpec as P

BLOCK = 128
REACH = 7
WIDE = REACH * BLOCK
SPAN = (2 * REACH + 1) * BLOCK
HALF = WIDE // 2
STEP = 448
CHUNK = 256
LOG2E = 1.4426950408889634
DEAD = -30000.0
F32 = jnp.float32
BF16 = jnp.bfloat16
MESH = pl.DeviceIdType.MESH


def pair_ones():
    row = lax.broadcasted_iota(jnp.int32, (256, 128), 0)
    col = lax.broadcasted_iota(jnp.int32, (256, 128), 1)
    return (((row // 64) % 2) == (col // 64)).astype(BF16)


def layer_normed(values, gain):
    center = jnp.mean(values, axis=-1, keepdims=True)
    shifted = values - center
    spread = jnp.mean(jnp.square(shifted), axis=-1, keepdims=True)
    return (shifted * lax.rsqrt(spread + 1e-05) * gain).astype(BF16)


def head_normed(raw, gain, ones):
    square = raw * raw
    high = square.astype(BF16)
    low = (square - high.astype(F32)).astype(BF16)
    total = jnp.dot(jnp.concatenate([high, low], 1), ones, preferred_element_type=F32)
    return (raw * lax.rsqrt(total * (1.0 / 64.0) + 1e-06) * gain).astype(BF16)


def rows_at(first, count):
    return pl.ds(pl.multiple_of(first, 64), count)


def attend_block(q, first_key, key_count, kv, first, lane):
    zero = jnp.zeros_like(q)
    live = (lane >= first_key) & (lane < first_key + key_count)
    bias = jnp.where(live, 0.0, DEAD).astype(BF16)
    both = jnp.concatenate(
        [
            jnp.concatenate([jnp.where(lane < 64, q, zero), bias], 1),
            jnp.concatenate([jnp.where(lane < 64, zero, q), bias], 1),
        ],
        0,
    )
    acc = None
    for j in range(0, SPAN, CHUNK):
        count = min(CHUNK, SPAN - j)
        marks = [(lane == (j // BLOCK + m)).astype(BF16) for m in range(count // BLOCK)]
        keys = jnp.concatenate([kv[rows_at(first + j, count), :128], jnp.concatenate(marks, 0)], 1)
        values = jnp.concatenate([kv[rows_at(first + j, count), 128:], jnp.ones((count, 128), BF16)], 1)
        scores = lax.dot_general(both, keys, (((1,), (1,)), ((), ())), preferred_element_type=F32)
        part = jnp.dot(jnp.exp2(scores).astype(BF16), values, preferred_element_type=F32)
        acc = part if acc is None else acc + part
    mixed = acc[:, :128] * (1.0 / acc[:, 128:])
    return jnp.where(lane < 64, mixed[:BLOCK], mixed[BLOCK:]).astype(BF16)


def layer(
    tok, ln, w_hbm, gain, ow_hbm, key_start, key_count, out,
    xv, w, wf, g, gf, ow, kv, qs, att, rcv, res,
    in_sem, w_sem, halo_send, halo_recv, give_send, give_recv, keep_sem, z_send, z_recv, xy_send, xy_recv,
):
    band = lax.axis_index("band")
    head = lax.axis_index("head")
    member = lax.axis_index("member")
    bands = 16
    line = band // 4
    x = band % 4
    t = head // 2
    c = head % 2
    t_op = (t + 2) % 4
    t_a = 1 + t % 2
    t_b = 3 * ((t + 1) % 2)
    far = t_op * 2 + c

    order = (3, 0, 1, 2)
    loads = {}
    for ch in order:
        loads[ch] = pltpu.make_async_copy(
            tok.at[pl.ds(ch * WIDE, WIDE), :], xv.at[pl.ds(ch * WIDE, WIDE), :], in_sem.at[ch]
        )
    loads[3].start()
    load_w = [
        pltpu.make_async_copy(w_hbm.at[p], w.at[:, pl.ds(p * 128, 128)], w_sem.at[p]) for p in range(3)
    ]
    for copy in load_w:
        copy.start()
    for ch in order[1:]:
        loads[ch].start()
    load_ow = pltpu.make_async_copy(ow_hbm, ow, w_sem.at[3])
    load_ow.start()
    load_res = pltpu.make_async_copy(tok.at[rows_at(t * WIDE + c * HALF, HALF), :], res, w_sem.at[4])
    load_res.start()

    barrier = pltpu.get_barrier_semaphore()
    for d in range(1, 8):
        pl.semaphore_signal(barrier, inc=1, device_id={"head": (head + d) % 8}, device_id_type=MESH)
    for d in range(1, 4):
        pl.semaphore_signal(barrier, inc=1, device_id={"band": line * 4 + (x + d) % 4}, device_id_type=MESH)
        pl.semaphore_signal(barrier, inc=1, device_id={"member": (member + d) % 4}, device_id_type=MESH)

    @pl.when(x == 3)
    def _():
        pl.semaphore_signal(barrier, inc=1, device_id={"band": (band + 1) % bands}, device_id_type=MESH)

    @pl.when(x == 0)
    def _():
        pl.semaphore_signal(barrier, inc=1, device_id={"band": (band + bands - 1) % bands}, device_id_type=MESH)

    @pl.when(band == 0)
    def _():
        kv[pl.ds(0, WIDE), :] = jnp.zeros((WIDE, 256), BF16)

    @pl.when(band == bands - 1)
    def _():
        kv[pl.ds(5 * WIDE, WIDE), :] = jnp.zeros((WIDE, 256), BF16)

    @pl.when((band == 0) & (t == 0))
    def _():
        kv[pl.ds(6 * WIDE, WIDE), :] = jnp.zeros((WIDE, 256), BF16)

    @pl.when((band == bands - 1) & (t == 3))
    def _():
        kv[pl.ds(8 * WIDE, WIDE), :] = jnp.zeros((WIDE, 256), BF16)

    ones = pair_ones()
    for kind in range(2):
        g[kind : kind + 1, :] = jnp.concatenate([gain[kind, 0:1, :], gain[kind, 1:2, :]], 1)
    g[2:8, :] = jnp.zeros((6, 128), F32)

    def put_kv(raw, gains, first):
        kv[rows_at(first, STEP), :128] = head_normed(raw[:, :128], gains[1:2, :], ones)
        kv[rows_at(first, STEP), 128:] = raw[:, 128:].astype(BF16)

    def put_q(raw, gains, first):
        qs[rows_at(first, STEP), :] = head_normed(raw, gains[0:1, :] * (LOG2E / 8.0), ones)

    def project(ch):
        def step(s, carry):
            first = ch * WIDE + s * STEP
            normed = layer_normed(xv[rows_at(first, STEP), :].astype(F32), ln[...])
            xv[rows_at(first, STEP), :] = normed
            raw = jnp.dot(normed, w[...], preferred_element_type=F32)
            put_q(raw[:, :128], g, first)
            put_kv(raw[:, 128:], g, WIDE + first)
            return carry

        lax.fori_loop(0, WIDE // STEP, step, 0)

    def project_far(ch, target):
        def step(s, carry):
            normed = xv[rows_at(ch * WIDE + s * STEP, STEP), :]
            raw = jnp.dot(normed, wf[:, 128:], preferred_element_type=F32)
            put_kv(raw, gf, target + s * STEP)
            return carry

        lax.fori_loop(0, WIDE // STEP, step, 0)

    def halo(side):
        return pltpu.make_async_remote_copy(
            src_ref=kv.at[pl.ds((4 - 3 * side) * WIDE, WIDE), :],
            dst_ref=kv.at[pl.ds(5 * side * WIDE, WIDE), :],
            send_sem=halo_send.at[side],
            recv_sem=halo_recv.at[side],
            device_id={"band": band + 1 - 2 * side},
            device_id_type=MESH,
        )

    def far_halo(side):
        return pltpu.make_async_remote_copy(
            src_ref=kv.at[pl.ds(9 * WIDE, WIDE), :],
            dst_ref=kv.at[pl.ds((6 + 2 * side) * WIDE, WIDE), :],
            send_sem=halo_send.at[2],
            recv_sem=halo_recv.at[2],
            device_id={"band": band + 1 - 2 * side},
            device_id_type=MESH,
        )

    piece = rows_at(64 * (4 * member + x), 64)
    quarter = rows_at(256 * member, 256)

    def send_z(which):
        return pltpu.make_async_remote_copy(
            src_ref=(w.at[piece, :], g)[which],
            dst_ref=(wf.at[piece, :], gf)[which],
            send_sem=z_send.at[which],
            recv_sem=z_recv.at[which],
            device_id={"head": far},
            device_id_type=MESH,
        )

    def send_x(d):
        return pltpu.make_async_remote_copy(
            src_ref=wf.at[piece, :],
            dst_ref=wf.at[piece, :],
            send_sem=xy_send.at[d - 1],
            recv_sem=xy_recv.at[d - 1],
            device_id={"band": line * 4 + (x + d) % 4},
            device_id_type=MESH,
        )

    def recv_x(d):
        came = rows_at(64 * (4 * member + (x + 4 - d) % 4), 64)
        return pltpu.make_async_remote_copy(
            src_ref=wf.at[came, :],
            dst_ref=wf.at[came, :],
            send_sem=xy_send.at[d - 1],
            recv_sem=xy_recv.at[d - 1],
            device_id={"band": line * 4 + (x + 4 - d) % 4},
            device_id_type=MESH,
        )

    def send_y(d):
        return pltpu.make_async_remote_copy(
            src_ref=wf.at[quarter, :],
            dst_ref=wf.at[quarter, :],
            send_sem=xy_send.at[d + 2],
            recv_sem=xy_recv.at[d + 2],
            device_id={"member": (member + d) % 4},
            device_id_type=MESH,
        )

    def recv_y(d):
        came = rows_at(256 * ((member + 4 - d) % 4), 256)
        return pltpu.make_async_remote_copy(
            src_ref=wf.at[came, :],
            dst_ref=wf.at[came, :],
            send_sem=xy_send.at[d + 2],
            recv_sem=xy_recv.at[d + 2],
            device_id={"member": (member + 4 - d) % 4},
            device_id_type=MESH,
        )

    loads[3].wait()
    for copy in load_w:
        copy.wait()
    project(3)
    pl.semaphore_wait(barrier, 13 + (x + 1) // 4 + (4 - x) // 4)
    send_z(0).start()
    send_z(1).start()

    @pl.when(band < bands - 1)
    def _():
        halo(0).start()

    loads[0].wait()
    project(0)

    @pl.when(band > 0)
    def _():
        halo(1).start()

    loads[1].wait()
    project(1)
    send_z(0).wait_recv()
    for d in (1, 3, 2):
        send_x(d).start()
    loads[2].wait()
    project(2)

    lane = lax.broadcasted_iota(jnp.int32, (BLOCK, 128), 1)

    def give(unit, part, chip, core, slot, column):
        return pltpu.make_async_remote_copy(
            src_ref=att.at[rows_at(unit * WIDE + part * HALF, HALF), :],
            dst_ref=rcv.at[:, pl.ds(pl.multiple_of(column * 128, 128), 128)],
            send_sem=give_send.at[slot],
            recv_sem=give_recv.at[column],
            device_id={"head": chip * 2 + core},
            device_id_type=MESH,
        )

    def block(unit, chip, i, q_first, kv_first):
        local = chip * REACH + i
        att[rows_at(unit * WIDE + i * BLOCK, BLOCK), :] = attend_block(
            qs[rows_at(q_first + i * BLOCK, BLOCK), :],
            key_start[local] - (band * 4 * REACH + local - REACH),
            key_count[local],
            kv,
            kv_first + i * BLOCK,
            lane,
        )

    for i in range(7):
        block(0, t_a, i, t_a * WIDE, t_a * WIDE)
        if i == 1:
            for d in (1, 3, 2):
                recv_x(d).wait_recv()
            for d in (1, 3, 2):
                send_y(d).start()
        if i == 3:
            give(0, 0, t_a, 0, 0, head).start()
    give(0, 1, t_a, 1, 1, head).start()

    @pl.when(band > 0)
    def _():
        halo(0).wait_recv()

    @pl.when(band < bands - 1)
    def _():
        halo(1).wait_recv()

    for i in range(7):
        block(1, t_b, i, t_b * WIDE, t_b * WIDE)
        if i == 3:
            give(1, 0, t_b, 0, 2, head).start()
    give(1, 1, t_b, 1, 3, head).start()

    for d in (1, 3, 2):
        recv_y(d).wait_recv()
    send_z(1).wait_recv()
    inner = ((t + 1) // 2) % 2
    edge = 2 * (t // 2)
    project_far(t_b, (9 - inner * (3 - edge)) * WIDE)

    @pl.when((t == 0) & (band < bands - 1))
    def _():
        far_halo(0).start()

    @pl.when((t == 3) & (band > 0))
    def _():
        far_halo(1).start()

    project_far(t_a, (8 - edge) * WIDE)
    project_far(t, 7 * WIDE)

    def far_queries(s, carry):
        raw = jnp.dot(xv[rows_at(t * WIDE + s * STEP, STEP), :], wf[:, :128], preferred_element_type=F32)
        put_q(raw, gf, 4 * WIDE + s * STEP)
        return carry

    lax.fori_loop(0, WIDE // STEP, far_queries, 0)

    def keep(unit, column, sem):
        return pltpu.make_async_copy(
            att.at[rows_at(unit * WIDE + c * HALF, HALF), :],
            rcv.at[:, pl.ds(pl.multiple_of(column * 128, 128), 128)],
            keep_sem.at[sem],
        )

    for k in range(7):
        block(2, t, (k + 3 * (1 - c)) % 7, t * WIDE, t * WIDE)
        if k == 3:
            give(2, 1 - c, t, 1 - c, 4, head).start()
    keep(2, head, 0).start()

    @pl.when((t == 0) & (band > 0))
    def _():
        far_halo(0).wait_recv()

    @pl.when((t == 3) & (band < bands - 1))
    def _():
        far_halo(1).wait_recv()

    for k in range(7):
        block(3, t, (k + 3 * (1 - c)) % 7, 4 * WIDE, 6 * WIDE)
        if k == 3:
            give(3, 1 - c, t, 1 - c, 5, far).start()
    keep(3, far, 1).start()

    load_ow.wait()
    load_res.wait()
    keep(2, head, 0).wait()
    keep(3, far, 1).wait()
    up = (t + 1) % 4
    down = (t + 3) % 4
    for column in (up * 2, up * 2 + 1, down * 2, down * 2 + 1, t * 2 + 1 - c, t_op * 2 + 1 - c):
        pltpu.make_async_remote_copy(
            src_ref=att.at[pl.ds(0, HALF), :],
            dst_ref=rcv.at[:, pl.ds(pl.multiple_of(column * 128, 128), 128)],
            send_sem=give_send.at[0],
            recv_sem=give_recv.at[column],
            device_id={"head": t * 2 + 1 - c},
            device_id_type=MESH,
        ).wait_recv()
    for r in range(0, HALF, 224):
        summed = jnp.dot(rcv[pl.ds(r, 224), :], ow[...], preferred_element_type=F32)
        out[pl.ds(r, 224), :] = (res[pl.ds(r, 224), :].astype(F32) + summed).astype(BF16)
    for slot in range(4):
        chip = (t_a, t_b)[slot // 2]
        give(slot // 2, slot % 2, chip, slot % 2, slot, head).wait_send()
    give(2, 1 - c, t, 1 - c, 4, head).wait_send()
    give(3, 1 - c, t, 1 - c, 5, far).wait_send()
    send_z(0).wait_send()
    send_z(1).wait_send()
    for d in (1, 2, 3):
        send_x(d).wait_send()
        send_y(d).wait_send()

    @pl.when(band < bands - 1)
    def _():
        halo(0).wait_send()

    @pl.when(band > 0)
    def _():
        halo(1).wait_send()

    @pl.when((t == 0) & (band < bands - 1))
    def _():
        far_halo(0).wait_send()

    @pl.when((t == 3) & (band > 0))
    def _():
        far_halo(1).wait_send()


def on_device(tokens, ln_gain, qkv_weight, qk_gain, out_weight, key_start, key_count):
    rows, features = tokens.shape
    columns = qk_gain.shape[1] * qk_gain.shape[2]
    weight = jnp.transpose(qkv_weight, (1, 0, 2))
    whole = pl.BlockSpec(memory_space=pltpu.VMEM)
    scalars = pl.BlockSpec(memory_space=pltpu.SMEM)
    far = pl.BlockSpec(memory_space=pl.ANY)
    return pl.pallas_call(
        layer,
        out_shape=jax.ShapeDtypeStruct((HALF, features), BF16),
        in_specs=[far, whole, far, whole, far, scalars, scalars],
        out_specs=whole,
        scratch_shapes=[
            pltpu.VMEM((rows, features), BF16),
            pltpu.VMEM((features, 3 * columns), BF16),
            pltpu.VMEM((features, 3 * columns), BF16),
            pltpu.VMEM((8, 128), F32),
            pltpu.VMEM((8, 128), F32),
            pltpu.VMEM((features, features), BF16),
            pltpu.VMEM((10 * WIDE, 256), BF16),
            pltpu.VMEM((5 * WIDE, 128), BF16),
            pltpu.VMEM((4 * WIDE, 128), BF16),
            pltpu.VMEM((HALF, features), BF16),
            pltpu.VMEM((HALF, features), BF16),
            pltpu.SemaphoreType.DMA((4,)),
            pltpu.SemaphoreType.DMA((5,)),
            pltpu.SemaphoreType.DMA((3,)),
            pltpu.SemaphoreType.DMA((3,)),
            pltpu.SemaphoreType.DMA((6,)),
            pltpu.SemaphoreType.DMA((8,)),
            pltpu.SemaphoreType.DMA((2,)),
            pltpu.SemaphoreType.DMA((2,)),
            pltpu.SemaphoreType.DMA((2,)),
            pltpu.SemaphoreType.DMA((6,)),
            pltpu.SemaphoreType.DMA((6,)),
        ],
        compiler_params=pltpu.CompilerParams(
            vmem_limit_bytes=56 << 20, collective_id=0, has_side_effects=True
        ),
        name="layer",
    )(tokens, ln_gain.reshape(1, features), weight, qk_gain, out_weight, key_start, key_count)


def solution(mesh):
    placed = (
        P(("member", "band"), None),
        P(),
        P(None, None, "head"),
        P(None, "head", None),
        P(),
        P("band"),
        P("band"),
    )
    return jax.shard_map(
        on_device,
        mesh=mesh,
        in_specs=placed,
        out_specs=P(("member", "band", "head"), None),
        check_vma=False,
    )
```

time: 86.2 us -> 76.3 us (0.89)
  the two profiles are of different devices: /device:TPU:1 before, /device:TPU:48 now
where the time goes in v3:
time: 76.3 us; the launch traced here: 76.1 us
  Pallas kernels  73.9 us (97%)
  local copies, waits for them, and re-layouts  2.16 us (3%)
    pallas_call x1, Pallas kernels, on_device(): pl.pallas_call(layer, out_shape=jax.ShapeDtypeStruct((HALF, features), BF...  73.9 us
    unnamed x1, local copies, waits for them, and re-layouts  2.16 us

profile of v3, /device:TPU:48, one launch (start us, length us, event | category | flops | bytes accessed | tf_op | source)
XLA Modules:
  0.0 76.1 jit_solution(7933229468528355148)
XLA Ops:
  0.0 73.9 %layer.1 = bf16[448,1024]{1,0:T(8,128)(2,1)} custom-call(bf16[3584,1024]{1,0:T(8,128)(2,1)} %tok.1, f32[1,1024]{1,0:T(1,128)} %bitcast.3, bf16[3,1024,128]{2,1,0:T(8,128)(2,1)} %bitcast.2, f32[2,2,64]{2,1,0:T(2,128)} %gain.1, bf16[1024,1024]{1,0:T(8,128)(2,1)} %ow_hbm.1, s32[28]{0:T(128)} %key_start.1, s32[28]{0:T(128)} %key_count.1), custom_call_target="tpu_custom_call" | custom-call | tf_op jit(solution)/shard_map/layer/pallas_call | solution.py:427
  73.9 2.2 %copy.9 = bf16[448,1024]{1,0:T(8,128)(2,1)} copy(bf16[448,1024]{1,0:T(8,128)(2,1)} %layer.1) | data formatting | bytes 1835008

commit v4 on v3

--- a/solution.py
+++ b/solution.py
@@ -68,9 +68,32 @@
     return jnp.where(lane < 64, mixed[:BLOCK], mixed[BLOCK:]).astype(BF16)
 
 
+def attend_part(q, first_key, key_count, kv, first, lane, count):
+    zero = jnp.zeros_like(q)
+    live = (lane >= first_key) & (lane < first_key + key_count)
+    bias = jnp.where(live, 0.0, DEAD).astype(BF16)
+    both = jnp.concatenate(
+        [
+            jnp.concatenate([jnp.where(lane < 64, q, zero), bias], 1),
+            jnp.concatenate([jnp.where(lane < 64, zero, q), bias], 1),
+        ],
+        0,
+    )
+    acc = None
+    for j in range(0, count * BLOCK, CHUNK):
+        size = min(CHUNK, count * BLOCK - j)
+        marks = [(lane == (j // BLOCK + m)).astype(BF16) for m in range(size // BLOCK)]
+        keys = jnp.concatenate([kv[rows_at(first + j, size), :128], jnp.concatenate(marks, 0)], 1)
+        values = jnp.concatenate([kv[rows_at(first + j, size), 128:], jnp.ones((size, 128), BF16)], 1)
+        scores = lax.dot_general(both, keys, (((1,), (1,)), ((), ())), preferred_element_type=F32)
+        part = jnp.dot(jnp.exp2(scores).astype(BF16), values, preferred_element_type=F32)
+        acc = part if acc is None else acc + part
+    return acc
+
+
 def layer(
     tok, ln, w_hbm, gain, ow_hbm, key_start, key_count, out,
-    xv, w, wf, g, gf, ow, kv, qs, att, rcv, res,
+    xv, w, wf, g, gf, ow, kv, qs, acc, total, att, rcv, res,
     in_sem, w_sem, halo_send, halo_recv, give_send, give_recv, keep_sem, z_send, z_recv, xy_send, xy_recv,
 ):
     band = lax.axis_index("band")
@@ -357,27 +380,30 @@
             give(2, 1 - c, t, 1 - c, 4, head).start()
     keep(2, head, 0).start()
 
-    @pl.when((t == 0) & (band > 0))
-    def _():
-        far_halo(0).wait_recv()
-
-    @pl.when((t == 3) & (band < bands - 1))
-    def _():
-        far_halo(1).wait_recv()
+    hi = t // 2
+
+    def part(k, count, base, skip):
+        i = k + hi * (6 - 2 * k)
+        local = t * REACH + i
+        return i, attend_part(
+            qs[rows_at(4 * WIDE + i * BLOCK, BLOCK), :],
+            key_start[local] - (band * 4 * REACH + local - REACH) - skip,
+            key_count[local],
+            kv,
+            6 * WIDE + base * BLOCK,
+            lane,
+            count,
+        )
 
     for k in range(7):
-        block(3, t, (k + 3 * (1 - c)) % 7, 4 * WIDE, 6 * WIDE)
-        if k == 3:
-            give(3, 1 - c, t, 1 - c, 5, far).start()
-    keep(3, far, 1).start()
+        _, sums = part(k, 8 + k, 7 * (1 - hi) + hi * (6 - k), (1 - hi) * (7 - k))
+        acc[pl.ds(k * 256, 256), :] = sums
 
     load_ow.wait()
     load_res.wait()
     keep(2, head, 0).wait()
-    keep(3, far, 1).wait()
-    up = (t + 1) % 4
-    down = (t + 3) % 4
-    for column in (up * 2, up * 2 + 1, down * 2, down * 2 + 1, t * 2 + 1 - c, t_op * 2 + 1 - c):
+
+    def arrive(column):
         pltpu.make_async_remote_copy(
             src_ref=att.at[pl.ds(0, HALF), :],
             dst_ref=rcv.at[:, pl.ds(pl.multiple_of(column * 128, 128), 128)],
@@ -386,9 +412,64 @@
             device_id={"head": t * 2 + 1 - c},
             device_id_type=MESH,
         ).wait_recv()
+
+    def out_part(chip, r):
+        columns = pl.ds(pl.multiple_of(chip * 256, 256), 256)
+        return jnp.dot(rcv[pl.ds(r, 224), columns], ow[columns, :], preferred_element_type=F32)
+
+    def edge_part(k):
+        i, sums = part(k, 7 - k, (1 - hi) * k + 14 * hi, hi * (8 + k))
+        sums = sums + acc[pl.ds(k * 256, 256), :]
+        mixed = sums[:, :128] * (1.0 / sums[:, 128:])
+        att[rows_at(3 * WIDE + i * BLOCK, BLOCK), :] = jnp.where(lane < 64, mixed[:BLOCK], mixed[BLOCK:]).astype(BF16)
+
+    def edges(ks):
+        for n, k in enumerate(ks):
+            edge_part(k)
+            if n == 3:
+                give(3, 1 - c, t, 1 - c, 5, far).start()
+
+    def first_parts():
+        up = (t + 1) % 4
+        down = (t + 3) % 4
+        for column in (t * 2 + 1 - c, up * 2, up * 2 + 1, down * 2, down * 2 + 1):
+            arrive(column)
+        for r in range(0, HALF, 224):
+            base = res[pl.ds(r, 224), :].astype(F32)
+            total[pl.ds(r, 224), :] = base + (out_part(t, r) + out_part(up, r) + out_part(down, r))
+
+    outer = (t == 0) | (t == 3)
+
+    @pl.when(outer)
+    def _():
+        first_parts()
+
+    @pl.when((t == 0) & (band > 0))
+    def _():
+        far_halo(0).wait_recv()
+
+    @pl.when((t == 3) & (band < bands - 1))
+    def _():
+        far_halo(1).wait_recv()
+
+    @pl.when((c + hi) % 2 == 1)
+    def _():
+        edges((0, 1, 2, 3, 4, 5, 6))
+
+    @pl.when((c + hi) % 2 == 0)
+    def _():
+        edges((6, 5, 4, 3, 2, 1, 0))
+
+    keep(3, far, 1).start()
+
+    @pl.when((t == 1) | (t == 2))
+    def _():
+        first_parts()
+
+    keep(3, far, 1).wait()
+    arrive(t_op * 2 + 1 - c)
     for r in range(0, HALF, 224):
-        summed = jnp.dot(rcv[pl.ds(r, 224), :], ow[...], preferred_element_type=F32)
-        out[pl.ds(r, 224), :] = (res[pl.ds(r, 224), :].astype(F32) + summed).astype(BF16)
+        out[pl.ds(r, 224), :] = (total[pl.ds(r, 224), :] + out_part(t_op, r)).astype(BF16)
     for slot in range(4):
         chip = (t_a, t_b)[slot // 2]
         give(slot // 2, slot % 2, chip, slot % 2, slot, head).wait_send()
@@ -438,6 +519,8 @@
             pltpu.VMEM((features, features), BF16),
             pltpu.VMEM((10 * WIDE, 256), BF16),
             pltpu.VMEM((5 * WIDE, 128), BF16),
+            pltpu.VMEM((REACH * 256, 256), F32),
+            pltpu.VMEM((HALF, features), F32),
             pltpu.VMEM((4 * WIDE, 128), BF16),
             pltpu.VMEM((HALF, features), BF16),
             pltpu.VMEM((HALF, features), BF16),

time: 76.3 us -> 73.2 us (0.959)
  the two profiles are of different devices: /device:TPU:48 before, /device:TPU:57 now
where the time goes in v4:
time: 73.2 us; the launch traced here: 73 us
  Pallas kernels  70.9 us (97%)
  local copies, waits for them, and re-layouts  2.16 us (3%)
    pallas_call x1, Pallas kernels, on_device(): pl.pallas_call(layer, out_shape=jax.ShapeDtypeStruct((HALF, features), BF...  70.9 us
    unnamed x1, local copies, waits for them, and re-layouts  2.16 us

profile of v4, /device:TPU:57, one launch (start us, length us, event | category | flops | bytes accessed | tf_op | source)
XLA Modules:
  0.0 73.0 jit_solution(1382170243894298575)
XLA Ops:
  0.0 70.9 %layer.1 = bf16[448,1024]{1,0:T(8,128)(2,1)} custom-call(bf16[3584,1024]{1,0:T(8,128)(2,1)} %tok.1, f32[1,1024]{1,0:T(1,128)} %bitcast.3, bf16[3,1024,128]{2,1,0:T(8,128)(2,1)} %bitcast.2, f32[2,2,64]{2,1,0:T(2,128)} %gain.1, bf16[1024,1024]{1,0:T(8,128)(2,1)} %ow_hbm.1, s32[28]{0:T(128)} %key_start.1, s32[28]{0:T(128)} %key_count.1), custom_call_target="tpu_custom_call" | custom-call | tf_op jit(solution)/shard_map/layer/pallas_call | solution.py:508
  70.9 2.2 %copy.9 = bf16[448,1024]{1,0:T(8,128)(2,1)} copy(bf16[448,1024]{1,0:T(8,128)(2,1)} %layer.1) | data formatting | bytes 1835008

commit v5 on v4

--- a/solution.py
+++ b/solution.py
@@ -275,14 +275,14 @@
     send_z(0).start()
     send_z(1).start()
 
-    @pl.when(band < bands - 1)
+    @pl.when((band < bands - 1) & (t != 2))
     def _():
         halo(0).start()
 
     loads[0].wait()
     project(0)
 
-    @pl.when(band > 0)
+    @pl.when((band > 0) & (t != 1))
     def _():
         halo(1).start()
 
@@ -328,11 +328,11 @@
             give(0, 0, t_a, 0, 0, head).start()
     give(0, 1, t_a, 1, 1, head).start()
 
-    @pl.when(band > 0)
+    @pl.when((band > 0) & (t != 2))
     def _():
         halo(0).wait_recv()
 
-    @pl.when(band < bands - 1)
+    @pl.when((band < bands - 1) & (t != 1))
     def _():
         halo(1).wait_recv()
 
@@ -481,11 +481,11 @@
         send_x(d).wait_send()
         send_y(d).wait_send()
 
-    @pl.when(band < bands - 1)
+    @pl.when((band < bands - 1) & (t != 2))
     def _():
         halo(0).wait_send()
 
-    @pl.when(band > 0)
+    @pl.when((band > 0) & (t != 1))
     def _():
         halo(1).wait_send()
 

time: 73.2 us -> 73.8 us (level)
  the two profiles are of different devices: /device:TPU:57 before, /device:TPU:33 now
where the time goes in v5:
time: 73.8 us; the launch traced here: 73.6 us
  Pallas kernels  71.4 us (97%)
  local copies, waits for them, and re-layouts  2.16 us (3%)
    pallas_call x1, Pallas kernels, on_device(): pl.pallas_call(layer, out_shape=jax.ShapeDtypeStruct((HALF, features), BF...  71.4 us
    unnamed x1, local copies, waits for them, and re-layouts  2.16 us

profile of v5, /device:TPU:33, one launch (start us, length us, event | category | flops | bytes accessed | tf_op | source)
XLA Modules:
  0.0 73.6 jit_solution(12356641283470883219)
XLA Ops:
  0.0 71.4 %layer.1 = bf16[448,1024]{1,0:T(8,128)(2,1)} custom-call(bf16[3584,1024]{1,0:T(8,128)(2,1)} %tok.1, f32[1,1024]{1,0:T(1,128)} %bitcast.3, bf16[3,1024,128]{2,1,0:T(8,128)(2,1)} %bitcast.2, f32[2,2,64]{2,1,0:T(2,128)} %gain.1, bf16[1024,1024]{1,0:T(8,128)(2,1)} %ow_hbm.1, s32[28]{0:T(128)} %key_start.1, s32[28]{0:T(128)} %key_count.1), custom_call_target="tpu_custom_call" | custom-call | tf_op jit(solution)/shard_map/layer/pallas_call | solution.py:508
  71.4 2.2 %copy.9 = bf16[448,1024]{1,0:T(8,128)(2,1)} copy(bf16[448,1024]{1,0:T(8,128)(2,1)} %layer.1) | data formatting | bytes 1835008
